TPU v7x, 32 devices: a whole 2x2x4 slice. The times are simulated.
32 devices in a mesh: head: 4 (over x, core), ctx: 8 (over z, y).
Axes of the slice: x: 2, y: 2, z: 4, core: 2. Of those that a mesh axis runs over, the one named last changes fastest.
Arguments:
- queries: bfloat16 [8192, 8192], P('ctx', 'head'), may hold values from -5 to 5
- keys: bfloat16 [8, 1024, 1024], P('ctx', 'head'), may hold values from -5 to 5
- values: bfloat16 [8, 1024, 1024], P('ctx', 'head'), may hold values from -6 to 6
- doc_ids: int32 [8192], P('ctx'), may hold values from 0 to 31, never falling along the last dimension, each value on 1 to 1024 neighbouring positions
- piece_owner: int32 [32], P('ctx'), may hold values from 0 to 7, as said below
Outputs:
- attended: bfloat16 [8192, 8192], P('ctx', 'head')
- owner_lse: float32 [8, 64, 2048], P('ctx', 'head')
Inputs may be any that keep to these rules, and one draw needn't show every extreme that they name: `piece_owner`: entry s * 4 + j names the owner of piece j of index s; the 4 entries of one index are distinct, and one owner is named by every index.
All inputs are finite; a program needn't handle non-finite values.
Results may differ from a plain program's by a relative error of at most 0.0046.
Values may be sent and summed in bfloat16 or wider, within the bound.
No kernel may reach another device: no remote copies, remote signals or barrier semaphores. Data moves between devices by JAX's collectives and lax.ppermute only.
A program may use at most 64 MiB of HBM per device.

v0:
```python
import math

import jax
import jax.numpy as jnp
from jax import lax
from jax.experimental import pallas as pl
from jax.experimental.pallas import tpu as pltpu
from jax.sharding import PartitionSpec as P

HEAD = 128
BLOCK = 256
INFO = 16
CODE = 32
NEG = -1e30
FLOOR = 60.0
CEILING = 90.0
SCALE2 = HEAD ** (-0.5) * math.log2(math.e)
LN2 = math.log(2.0)
VMEM_LIMIT = 50 * 1024 * 1024
NT = (((1,), (1,)), ((), ()))
NN = (((1,), (0,)), ((), ()))
IN_VMEM = pl.BlockSpec(memory_space=pltpu.VMEM)
IN_SMEM = pl.BlockSpec(memory_space=pltpu.SMEM)
IN_HBM = pl.BlockSpec(memory_space=pltpu.HBM)


def f32_dot(a, b, dims):
    return lax.dot_general(a, b, dims, preferred_element_type=jnp.float32)


def eye_rows(column):
    eye = lax.broadcasted_iota(jnp.int32, (HEAD, HEAD), 0) == lax.broadcasted_iota(jnp.int32, (HEAD, HEAD), 1)
    parts = [
        jnp.sum(jnp.where(eye, column[i : i + HEAD], 0.0), axis=0, keepdims=True)
        for i in range(0, column.shape[0], HEAD)
    ]
    return jnp.concatenate(parts, axis=1)


def row_column(row):
    return jnp.broadcast_to(row, (HEAD, row.shape[1])).T


def count(flags):
    return jnp.sum(flags.astype(jnp.int32))


def tile_of(ref, turn):
    return ref.at[pl.ds(pl.multiple_of(turn * BLOCK, BLOCK), BLOCK), :]


def prep_kernel(size, k_ref, v_ref, docs_ref, own_ref, *next_refs):
    here = lax.axis_index("head")
    rows, cols = k_ref.shape[1], k_ref.shape[2] // size
    for j in range(size):
        own_ref[j, :rows] = k_ref[0, :, j * cols : (j + 1) * cols]
        own_ref[j, rows:] = v_ref[0, :, j * cols : (j + 1) * cols]
    docs = docs_ref[...]
    last = docs[:, docs.shape[1] - 1 :]
    run = jnp.sum(jnp.where(docs == last, 1.0, 0.0), axis=1, keepdims=True)
    high = jnp.floor(run * (1.0 / CODE))
    line = lax.broadcasted_iota(jnp.int32, (INFO, cols), 0)
    info = jnp.where(line == 0, last.astype(jnp.float32), jnp.where(line == 1, high, run - high * CODE))
    info = info.astype(k_ref.dtype)
    for m in range(size):
        start = pl.multiple_of(lax.rem(here + m, size) * cols, cols)
        next_refs[m][:rows] = k_ref[0, :, pl.ds(start, cols)]
        next_refs[m][rows : 2 * rows] = v_ref[0, :, pl.ds(start, cols)]
        next_refs[m][2 * rows :] = info


def prep(keys, values, docs, size):
    _, rows, width = keys.shape
    cols = width // size
    own = jax.ShapeDtypeStruct((size, 2 * rows, cols), keys.dtype)
    onward = jax.ShapeDtypeStruct((2 * rows + INFO, cols), keys.dtype)

    def kernel(*refs):
        prep_kernel(size, *refs)

    return pl.pallas_call(
        kernel,
        out_shape=(own,) + (onward,) * size,
        in_specs=[IN_VMEM] * 3,
        out_specs=(IN_VMEM,) * (size + 1),
        cost_estimate=pl.CostEstimate(flops=0, bytes_accessed=12 * keys.size, transcendentals=0),
    )(keys, values, docs)


def own_kernel(q_ref, kv_ref, docs_ref, o_ref, l_ref, k_ref, vx_ref, bias_ref, first_ref):
    turn = pl.program_id(1)
    parts, rows = kv_ref.shape[0], kv_ref.shape[1] // 2
    tok = parts * rows
    turns = tok // BLOCK
    share = q_ref.shape[1] // HEAD

    @pl.when(turn == 0)
    def _():
        for j in range(parts):
            k_ref[j * rows : (j + 1) * rows] = kv_ref[j, :rows]
            vx_ref[j * rows : (j + 1) * rows, :HEAD] = kv_ref[j, rows:]
            vx_ref[j * rows : (j + 1) * rows, HEAD:] = jnp.ones((rows, HEAD), vx_ref.dtype)

    @pl.when((turn == 0) & (pl.program_id(0) == 0))
    def _():
        docs = docs_ref[...]
        for t in range(turns):
            first_ref[t] = count(docs < docs[:, t * BLOCK : t * BLOCK + 1]) // BLOCK

    first = first_ref[turn]
    for n in range(1, turns + 1):

        @pl.when(turn - first + 1 == n)
        def _(n=n):
            width = n * BLOCK
            base = pl.multiple_of(first * BLOCK, BLOCK)
            here = pl.multiple_of(turn * BLOCK, BLOCK)
            q_docs = row_column(docs_ref[:, pl.ds(here, BLOCK)])
            k_docs = docs_ref[:, pl.ds(base, width)]
            ahead = lax.broadcasted_iota(jnp.int32, (BLOCK, width), 1) - lax.broadcasted_iota(
                jnp.int32, (BLOCK, width), 0
            )
            keep = (jnp.concatenate([q_docs] * (width // HEAD), axis=1) == k_docs) & (ahead <= width - BLOCK)
            bias_ref[:, :width] = jnp.where(keep, 0.0, NEG)
            k = k_ref[pl.ds(base, width), :]
            vx = vx_ref[pl.ds(base, width), :]
            for h in range(share):
                lanes = slice(h * HEAD, (h + 1) * HEAD)
                s = f32_dot(q_ref[:, lanes], k, NT) * SCALE2 + bias_ref[:, :width]
                got = f32_dot(jnp.exp2(s).astype(jnp.bfloat16), vx, NN)
                total = got[:, HEAD:]
                o_ref[:, lanes] = (got[:, :HEAD] / total).astype(o_ref.dtype)
                l_ref[h : h + 1, :] = eye_rows(jnp.log2(total))


def own_part(queries, kv, docs):
    tok, width = queries.shape
    parts, twice, cols = kv.shape
    groups = cols // HEAD
    turns = tok // BLOCK
    share = width // HEAD // groups
    return pl.pallas_call(
        own_kernel,
        grid=(groups, turns),
        in_specs=[
            pl.BlockSpec((BLOCK, share * HEAD), lambda g, t: (t, g)),
            pl.BlockSpec((parts, twice, HEAD), lambda g, t: (0, 0, g)),
            pl.BlockSpec((1, tok), lambda g, t: (0, 0)),
        ],
        out_specs=(
            pl.BlockSpec((BLOCK, share * HEAD), lambda g, t: (t, g)),
            pl.BlockSpec((share, BLOCK), lambda g, t: (g, t)),
        ),
        out_shape=(
            jax.ShapeDtypeStruct((tok, width), jnp.bfloat16),
            jax.ShapeDtypeStruct((width // HEAD, tok), jnp.float32),
        ),
        scratch_shapes=[
            pltpu.VMEM((tok, HEAD), jnp.bfloat16),
            pltpu.VMEM((tok, 2 * HEAD), jnp.bfloat16),
            pltpu.VMEM((BLOCK, tok), jnp.float32),
            pltpu.SMEM((turns,), jnp.int32),
        ],
        compiler_params=pltpu.CompilerParams(vmem_limit_bytes=VMEM_LIMIT),
        cost_estimate=pl.CostEstimate(
            flops=4 * tok * tok * width, bytes_accessed=4 * tok * width, transcendentals=tok * tok * width // HEAD // 2
        ),
    )(queries, kv, docs)


def beyond(logs):
    return jnp.logical_not((logs > -FLOOR) & (logs < CEILING))


def rest_kernel(size, owner_ref, q_hbm, lown_ref, docs_ref, kv_ref, *refs):
    old_refs = refs[:size]
    done_hbm, o_hbm, send_ref, q_ref, o_ref, k_ref, vx_ref, new_ref, l_ref, acc_ref, top_ref = refs[size : size + 11]
    q_sem, d_sem, o_sem = refs[size + 11 :]
    del done_hbm
    turns = q_ref.shape[0]
    groups = vx_ref.shape[0]
    heads = q_ref.shape[2] // HEAD
    share = heads // groups
    rows = (old_refs[0].shape[0] - INFO) // 2
    tok = turns * BLOCK

    info = old_refs[0][2 * rows :, :HEAD].astype(jnp.float32)
    docs = docs_ref[...]
    same = info[0:1] == docs[:, :1].astype(jnp.float32)
    ahead = jnp.max(jnp.where(same, info[1:2] * CODE + info[2:3], 0.0)).astype(jnp.int32)
    behind = count(docs == docs[:, :1])
    steps = jnp.where(ahead > 0, (behind + BLOCK - 1) // BLOCK, 0)

    def q_copy(turn):
        return pltpu.make_async_copy(tile_of(q_hbm, turn), q_ref.at[turn], q_sem.at[turn])

    def d_copy(turn):
        return pltpu.make_async_copy(tile_of(o_hbm, turn), o_ref.at[turn], d_sem.at[turn])

    def o_copy(turn):
        return pltpu.make_async_copy(o_ref.at[turn], tile_of(o_hbm, turn), o_sem.at[turn])

    for turn in range(turns):

        @pl.when(turn < steps)
        def _(turn=turn):
            q_copy(turn).start()
            d_copy(turn).start()

    new_ref[...] = jnp.zeros(new_ref.shape, jnp.float32)
    here = lax.axis_index("head")
    for m in range(size):
        base = pl.multiple_of(lax.rem(here + size - m, size) * rows, rows)
        for g in range(groups):
            lanes = slice(g * HEAD, (g + 1) * HEAD)
            k_ref[g, pl.ds(base, rows), :] = old_refs[m][:rows, lanes]
            vx_ref[g, pl.ds(base, rows), :HEAD] = old_refs[m][rows : 2 * rows, lanes]
            vx_ref[g, pl.ds(base, rows), HEAD:] = jnp.ones((rows, HEAD), vx_ref.dtype)

    def one(turn, _):
        q_copy(turn).wait()
        d_copy(turn).wait()
        start = pl.multiple_of(turn * BLOCK, BLOCK)
        inside = start + lax.broadcasted_iota(jnp.int32, (BLOCK, HEAD), 0) < behind
        for n in range(1, turns + 1):

            @pl.when((ahead + BLOCK - 1) // BLOCK == n)
            def _(n=n):
                width = n * BLOCK
                place = lax.broadcasted_iota(jnp.int32, (1, width), 1)
                bias = jnp.where(place >= width - ahead, 0.0, NEG)

                def one_group(g, _):
                    k = k_ref[g, tok - width :, :]
                    vx = vx_ref[g, tok - width :, :]
                    top_head = pl.multiple_of(g * share, share)
                    weights = jnp.exp2(lown_ref[pl.ds(top_head, share), pl.ds(start, BLOCK)])
                    found = []
                    for h in range(share):
                        lanes = pl.ds(pl.multiple_of((g * share + h) * HEAD, HEAD), HEAD)
                        s = f32_dot(q_ref[turn, :, lanes], k, NT) * SCALE2 + bias
                        got = f32_dot(jnp.exp2(s).astype(jnp.bfloat16), vx, NN)
                        total = jnp.where(inside, got[:, HEAD:], 0.0)
                        before = o_ref[turn, :, lanes].astype(jnp.float32)
                        weight = row_column(weights[h : h + 1])
                        mixed = (before * weight + got[:, :HEAD]) / (weight + total)
                        o_ref[turn, :, lanes] = jnp.where(inside, mixed, before).astype(o_ref.dtype)
                        found.append(eye_rows(total))
                    new_ref[pl.ds(top_head, share), pl.ds(start, BLOCK)] = jnp.concatenate(found, axis=0)
                    return 0

                lax.fori_loop(0, groups, one_group, 0)

        o_copy(turn).start()
        return 0

    lax.fori_loop(0, steps, one, 0)
    own = lown_ref[...]
    new = new_ref[...]
    l_ref[...] = jnp.log2(jnp.exp2(own) + new)
    token = lax.broadcasted_iota(jnp.int32, (heads, tok), 1)
    met = (token < behind) & (ahead > 0)
    bad = count(beyond(own) | (met & beyond(jnp.log2(new))))
    for turn in range(turns):

        @pl.when(turn < steps)
        def _(turn=turn):
            o_copy(turn).wait()

    @pl.when(bad > 0)
    def _():
        def every(turn, _):
            q_copy(turn).start()
            q_copy(turn).wait()
            start = pl.multiple_of(turn * BLOCK, BLOCK)
            q_docs = row_column(docs_ref[:, pl.ds(start, BLOCK)])
            q_docs = jnp.concatenate([q_docs] * (BLOCK // HEAD), axis=1)
            row = start + lax.broadcasted_iota(jnp.int32, (BLOCK, BLOCK), 0)
            column = lax.broadcasted_iota(jnp.int32, (BLOCK, BLOCK), 1)

            def one_head(h, _):
                g = h // share
                lanes = pl.ds(pl.multiple_of(h * HEAD, HEAD), HEAD)
                q = q_ref[turn, :, lanes]
                acc_ref[...] = jnp.zeros(acc_ref.shape, jnp.float32)
                top_ref[...] = jnp.full(top_ref.shape, NEG, jnp.float32)

                def add(keep, k, v):
                    s = jnp.where(keep, f32_dot(q, k, NT) * SCALE2, NEG)
                    before = top_ref[...]
                    top = jnp.maximum(before, jnp.max(s, axis=1, keepdims=True))
                    shift = jnp.exp2(before - top)
                    p = jnp.where(keep, jnp.exp2(s - jnp.concatenate([top] * (BLOCK // HEAD), axis=1)), 0.0)
                    p = p.astype(jnp.bfloat16)
                    ones = jnp.ones(v.shape, v.dtype)
                    acc_ref[:, :HEAD] = acc_ref[:, :HEAD] * shift + f32_dot(p, v, NN)
                    acc_ref[:, HEAD:] = acc_ref[:, HEAD:] * shift + f32_dot(p, ones, NN)
                    top_ref[...] = top

                def old_block(j, _):
                    at = pl.multiple_of(j * BLOCK, BLOCK)
                    keep = (j * BLOCK + column >= tok - ahead) & (row < behind)
                    add(keep, k_ref[g, pl.ds(at, BLOCK), :], vx_ref[g, pl.ds(at, BLOCK), :HEAD])
                    return 0

                def own_block(j, _):
                    at = pl.multiple_of(j * BLOCK, BLOCK)
                    keep = (q_docs == docs_ref[:, pl.ds(at, BLOCK)]) & (j * BLOCK + column <= row)
                    per = BLOCK // rows
                    group = pl.ds(pl.multiple_of(g * HEAD, HEAD), HEAD)
                    k = jnp.concatenate([kv_ref[j * per + i, :rows, group] for i in range(per)], axis=0)
                    v = jnp.concatenate([kv_ref[j * per + i, rows:, group] for i in range(per)], axis=0)
                    add(keep, k, v)
                    return 0

                lax.fori_loop(0, turns, old_block, 0)
                lax.fori_loop(0, turn + 1, own_block, 0)
                total = acc_ref[:, HEAD:]
                o_ref[turn, :, lanes] = (acc_ref[:, :HEAD] / total).astype(o_ref.dtype)
                l_ref[pl.ds(h, 1), pl.ds(start, BLOCK)] = eye_rows(top_ref[...] + jnp.log2(total))
                return 0

            lax.fori_loop(0, heads, one_head, 0)
            o_copy(turn).start()
            o_copy(turn).wait()
            return 0

        lax.fori_loop(0, turns, every, 0)

    owners, _, piece = send_ref.shape
    for o in range(owners):
        found = jnp.zeros(send_ref.shape[1:], jnp.float32)
        for j in range(tok // piece):
            found = jnp.where(owner_ref[j] == o, l_ref[:, j * piece : (j + 1) * piece] * LN2, found)
        send_ref[o] = found


def rest_part(owner, queries, lown, docs, kv, old, done, owners, piece):
    tok, width = queries.shape
    size = len(old)
    heads = width // HEAD
    groups = old[0].shape[1] // HEAD
    turns = tok // BLOCK

    def kernel(*refs):
        rest_kernel(size, *refs)

    return pl.pallas_call(
        kernel,
        in_specs=[IN_SMEM, IN_HBM, IN_VMEM, IN_VMEM, IN_VMEM] + [IN_VMEM] * size + [IN_HBM],
        out_specs=(IN_HBM, IN_VMEM),
        out_shape=(
            jax.ShapeDtypeStruct((tok, width), jnp.bfloat16),
            jax.ShapeDtypeStruct((owners, heads, piece), jnp.float32),
        ),
        input_output_aliases={5 + size: 0},
        scratch_shapes=[
            pltpu.VMEM((turns, BLOCK, width), jnp.bfloat16),
            pltpu.VMEM((turns, BLOCK, width), jnp.bfloat16),
            pltpu.VMEM((groups, tok, HEAD), jnp.bfloat16),
            pltpu.VMEM((groups, tok, 2 * HEAD), jnp.bfloat16),
            pltpu.VMEM((heads, tok), jnp.float32),
            pltpu.VMEM((heads, tok), jnp.float32),
            pltpu.VMEM((BLOCK, 2 * HEAD), jnp.float32),
            pltpu.VMEM((BLOCK, HEAD), jnp.float32),
            pltpu.SemaphoreType.DMA((turns,)),
            pltpu.SemaphoreType.DMA((turns,)),
            pltpu.SemaphoreType.DMA((turns,)),
        ],
        compiler_params=pltpu.CompilerParams(vmem_limit_bytes=VMEM_LIMIT),
        cost_estimate=pl.CostEstimate(
            flops=tok * tok * width, bytes_accessed=4 * tok * width, transcendentals=tok * tok * heads // 4
        ),
    )(owner, queries, lown, docs, kv, *old, done)


def spread_kernel(x_ref, o_ref):
    owners, _, piece = x_ref.shape
    for i in range(owners):
        o_ref[0, :, i * piece : (i + 1) * piece] = x_ref[i]


def spread(got):
    owners, heads, piece = got.shape
    return pl.pallas_call(
        spread_kernel,
        out_shape=jax.ShapeDtypeStruct((1, heads, owners * piece), got.dtype),
        cost_estimate=pl.CostEstimate(flops=0, bytes_accessed=8 * got.size, transcendentals=0),
    )(got)


def per_device(queries, keys, values, doc_ids, piece_owner):
    ctx_size, head_size = lax.axis_size("ctx"), lax.axis_size("head")
    tok, _ = queries.shape
    piece = 2 * tok // ctx_size
    docs = doc_ids.reshape(1, tok)

    own_send, *next_send = prep(keys, values, docs, head_size)
    kv = lax.all_to_all(own_send, "head", 0, 0, tiled=True)
    old = []
    for m in range(head_size):
        route = [
            (h * ctx_size + i, (h + m) % head_size * ctx_size + i + 1)
            for h in range(head_size)
            for i in range(ctx_size - 1)
        ]
        old.append(lax.ppermute(next_send[m], ("head", "ctx"), route))

    done, lown = own_part(queries, kv, docs)
    attended, send = rest_part(piece_owner, queries, lown, docs, kv, old, done, ctx_size, piece)
    got = lax.all_to_all(send, "ctx", 0, 0, tiled=True)
    return attended, spread(got)


def solution(mesh):
    return jax.shard_map(
        per_device,
        mesh=mesh,
        in_specs=(
            P("ctx", "head"),
            P("ctx", "head", None),
            P("ctx", "head", None),
            P("ctx"),
            P("ctx"),
        ),
        out_specs=(P("ctx", "head"), P("ctx", "head", None)),
        check_vma=False,
    )
```

profile of v0, /device:TPU:0, one launch (start us, length us, event | category | flops | bytes accessed | tf_op | source)
XLA Modules:
  0.0 287.7 jit_solution(10364508245002740075)
XLA Ops:
  0.6 2.7 shard_map.68
  3.3 4.2 %all-to-all-start = ((bf16[4,512,256]{2,1,0:T(8,128)(2,1)}), bf16[4,512,256]{2,1,0:T(8,128)(2,1)S(1)}, u32[]{:S(2)}, u32[]{:S(2)}) async-start(bf16[4,512,256]{2,1,0:T(8,128)(2,1)} %get-tuple-element.11), calls=%async_computation | async-start | bytes 2097152 | tf_op jit(solution)/shard_map/all_to_all | solution.py:399
  7.6 4.2 %collective-permute-start = (bf16[528,256]{1,0:T(8,128)(2,1)}, bf16[528,256]{1,0:T(8,128)(2,1)S(1)}, u32[]{:S(2)}, u32[]{:S(2)}) collective-permute-start(bf16[528,256]{1,0:T(8,128)(2,1)} %get-tuple-element.13), channel_id=1, source_target_pairs={{0,1},{1,2},{2,3},{3,4},{4,5},{5,6},{6,7},{8,9},{9,10},{10,11},{11... | collective-permute-start | bytes 811016 | tf_op jit(solution)/shard_map/ppermute | solution.py:407
  11.8 3.2 %collective-permute-start.1 = (bf16[528,256]{1,0:T(8,128)(2,1)}, bf16[528,256]{1,0:T(8,128)(2,1)S(1)}, u32[]{:S(2)}, u32[]{:S(2)}) collective-permute-start(bf16[528,256]{1,0:T(8,128)(2,1)} %get-tuple-element.14), channel_id=1, source_target_pairs={{0,9},{1,10},{2,11},{3,12},{4,13},{5,14},{6,15},{8,17},{9,18},{10,... | collective-permute-start | bytes 811016 | tf_op jit(solution)/shard_map/ppermute | solution.py:407
  15.0 4.5 %collective-permute-start.2 = (bf16[528,256]{1,0:T(8,128)(2,1)}, bf16[528,256]{1,0:T(8,128)(2,1)S(1)}, u32[]{:S(2)}, u32[]{:S(2)}) collective-permute-start(bf16[528,256]{1,0:T(8,128)(2,1)} %get-tuple-element.15), channel_id=1, source_target_pairs={{0,17},{1,18},{2,19},{3,20},{4,21},{5,22},{6,23},{8,25},{9,26},{10... | collective-permute-start | bytes 811016 | tf_op jit(solution)/shard_map/ppermute | solution.py:407
  19.5 0.0 copy-start.1
  19.5 4.3 %collective-permute-start.3 = (bf16[528,256]{1,0:T(8,128)(2,1)}, bf16[528,256]{1,0:T(8,128)(2,1)S(1)}, u32[]{:S(2)}, u32[]{:S(2)}) collective-permute-start(bf16[528,256]{1,0:T(8,128)(2,1)} %get-tuple-element.16), channel_id=1, source_target_pairs={{0,25},{1,26},{2,27},{3,28},{4,29},{5,30},{6,31},{8,1},{9,2},{10,3... | collective-permute-start | bytes 811016 | tf_op jit(solution)/shard_map/ppermute | solution.py:407
  23.8 0.0 all-to-all-done.kv_ref.refs_4_
  23.8 0.0 copy-start
  23.8 0.7 copy-done
  24.5 13.4 %shard_map.69 = (bf16[1024,2048]{1,0:T(8,128)(2,1)}, f32[16,1024]{1,0:T(8,128)S(1)}) custom-call(bf16[1024,2048]{1,0:T(8,128)(2,1)} %refs_1_.3, bf16[4,512,256]{2,1,0:T(8,128)(2,1)S(1)} %all-to-all-done.kv_ref.refs_4_, s32[1,1024]{1,0:T(1,128)S(1)} %bitcast.2), custom_call_target="tpu_custom_call" | custom-call | flops 8589934592 | bytes 8388608 | tf_op jit(solution)/shard_map/pallas_call | solution.py:142
  37.9 0.0 collective-permute-done.refs_5_
  37.9 0.0 collective-permute-done.1.refs_6_
  37.9 0.0 collective-permute-done.2.refs_7_
  37.9 0.0 collective-permute-done.3.refs_8_
  37.9 0.0 copy-done.1
  37.9 225.0 %shard_map.70 = (bf16[1024,2048]{1,0:T(8,128)(2,1)}, f32[8,16,256]{2,1,0:T(8,128)S(1)}) custom-call(s32[4]{0:T(128)S(1)} %copy-done.1, bf16[1024,2048]{1,0:T(8,128)(2,1)} %refs_1_.3, f32[16,1024]{1,0:T(8,128)S(1)} %get-tuple-element.12.refs_2_, s32[1,1024]{1,0:T(1,128)S(1)} %bitcast.3, ...), custom_call_target="tpu_custom_call", output_to_operand_aliasing={{0}: (9, {})} | custom-call | flops 2147483648 | bytes 8388608 | tf_op jit(solution)/shard_map/pallas_call | solution.py:348
  262.9 23.2 %all_to_all.10.x_ref = f32[8,16,256]{2,1,0:T(8,128)} all-to-all(f32[8,16,256]{2,1,0:T(8,128)S(1)} %get-tuple-element.19), channel_id=1, replica_groups=mesh['head'=4,'ctx'=8] {'ctx'}, dimensions={0} | all-to-all | bytes 262144 | tf_op jit(solution)/shard_map/all_to_all | solution.py:411
  286.2 1.6 shard_map.71
Async XLA Ops:
  3.3 20.5 %all-to-all-start = ((bf16[4,512,256]{2,1,0:T(8,128)(2,1)}), bf16[4,512,256]{2,1,0:T(8,128)(2,1)S(1)}, u32[]{:S(2)}, u32[]{:S(2)}) async-start(bf16[4,512,256]{2,1,0:T(8,128)(2,1)} %get-tuple-element.11), calls=%async_computation | async-start | bytes 2097152 | tf_op jit(solution)/shard_map/all_to_all | solution.py:399
  7.6 30.3 %collective-permute-start = (bf16[528,256]{1,0:T(8,128)(2,1)}, bf16[528,256]{1,0:T(8,128)(2,1)S(1)}, u32[]{:S(2)}, u32[]{:S(2)}) collective-permute-start(bf16[528,256]{1,0:T(8,128)(2,1)} %get-tuple-element.13), channel_id=1, source_target_pairs={{0,1},{1,2},{2,3},{3,4},{4,5},{5,6},{6,7},{8,9},{9,10},{10,11},{11... | collective-permute-start | bytes 811016 | tf_op jit(solution)/shard_map/ppermute | solution.py:407
  11.8 26.1 %collective-permute-start.1 = (bf16[528,256]{1,0:T(8,128)(2,1)}, bf16[528,256]{1,0:T(8,128)(2,1)S(1)}, u32[]{:S(2)}, u32[]{:S(2)}) collective-permute-start(bf16[528,256]{1,0:T(8,128)(2,1)} %get-tuple-element.14), channel_id=1, source_target_pairs={{0,9},{1,10},{2,11},{3,12},{4,13},{5,14},{6,15},{8,17},{9,18},{10,... | collective-permute-start | bytes 811016 | tf_op jit(solution)/shard_map/ppermute | solution.py:407
  15.0 22.9 %collective-permute-start.2 = (bf16[528,256]{1,0:T(8,128)(2,1)}, bf16[528,256]{1,0:T(8,128)(2,1)S(1)}, u32[]{:S(2)}, u32[]{:S(2)}) collective-permute-start(bf16[528,256]{1,0:T(8,128)(2,1)} %get-tuple-element.15), channel_id=1, source_target_pairs={{0,17},{1,18},{2,19},{3,20},{4,21},{5,22},{6,23},{8,25},{9,26},{10... | collective-permute-start | bytes 811016 | tf_op jit(solution)/shard_map/ppermute | solution.py:407
  19.5 18.4 %copy-start.1 = (s32[4]{0:T(128)S(1)}, s32[4]{0:T(128)}, u32[]{:S(2)}) copy-start(s32[4]{0:T(128)} %refs_0_.3) | copy-start | bytes 52
  19.5 18.4 %collective-permute-start.3 = (bf16[528,256]{1,0:T(8,128)(2,1)}, bf16[528,256]{1,0:T(8,128)(2,1)S(1)}, u32[]{:S(2)}, u32[]{:S(2)}) collective-permute-start(bf16[528,256]{1,0:T(8,128)(2,1)} %get-tuple-element.16), channel_id=1, source_target_pairs={{0,25},{1,26},{2,27},{3,28},{4,29},{5,30},{6,31},{8,1},{9,2},{10,3... | collective-permute-start | bytes 811016 | tf_op jit(solution)/shard_map/ppermute | solution.py:407
  23.8 0.7 copy-start
where the time goes:
time: 288 us
  Pallas kernels  243 us (84%)
  blocking collectives  23.2 us (8%)
  starting transfers between devices  20.4 us (7%)
    pallas_call x1, Pallas kernels, rest_part(): pl.pallas_call(kernel, in_specs=[IN_SMEM, IN_HBM, IN_VMEM, IN_VMEM, IN_VM...  225 us
    all_to_all x1, blocking collectives, per_device(): got = lax.all_to_all(send, 'ctx', 0, 0, tiled=True)  23.2 us
    ppermute x4, starting transfers between devices, per_device(): old.append(lax.ppermute(next_send[m], ('head', 'ctx'), route))  16.2 us
    pallas_call x1, Pallas kernels, own_part(): pl.pallas_call(own_kernel, grid=(groups, turns), in_specs=[pl.BlockSpec((...  13.4 us
  transfers between devices with their start and end apart: 5, of which 0 were waited for; matrix products, arithmetic and copies ran while one was open for 0% of the time, Pallas kernels for 5%

commit v1 on v0

--- a/solution.py
+++ b/solution.py
@@ -1,3 +1,4 @@
+import itertools
 import math
 
 import jax
@@ -52,9 +53,6 @@
 def prep_kernel(size, k_ref, v_ref, docs_ref, own_ref, *next_refs):
     here = lax.axis_index("head")
     rows, cols = k_ref.shape[1], k_ref.shape[2] // size
-    for j in range(size):
-        own_ref[j, :rows] = k_ref[0, :, j * cols : (j + 1) * cols]
-        own_ref[j, rows:] = v_ref[0, :, j * cols : (j + 1) * cols]
     docs = docs_ref[...]
     last = docs[:, docs.shape[1] - 1 :]
     run = jnp.sum(jnp.where(docs == last, 1.0, 0.0), axis=1, keepdims=True)
@@ -62,8 +60,17 @@
     line = lax.broadcasted_iota(jnp.int32, (INFO, cols), 0)
     info = jnp.where(line == 0, last.astype(jnp.float32), jnp.where(line == 1, high, run - high * CODE))
     info = info.astype(k_ref.dtype)
+    ids = docs.astype(jnp.float32)
+    table = jnp.zeros((INFO, cols), jnp.float32)
+    for i in range(docs.shape[1] // cols):
+        table = jnp.where(line == i, ids[:, i * cols : (i + 1) * cols], table)
+    table = table.astype(k_ref.dtype)
+    for j in range(size):
+        own_ref[j, :rows] = k_ref[0, :, j * cols : (j + 1) * cols]
+        own_ref[j, rows : 2 * rows] = v_ref[0, :, j * cols : (j + 1) * cols]
+        own_ref[j, 2 * rows :] = table
     for m in range(size):
-        start = pl.multiple_of(lax.rem(here + m, size) * cols, cols)
+        start = pl.multiple_of(jnp.bitwise_xor(here, m) * cols, cols)
         next_refs[m][:rows] = k_ref[0, :, pl.ds(start, cols)]
         next_refs[m][rows : 2 * rows] = v_ref[0, :, pl.ds(start, cols)]
         next_refs[m][2 * rows :] = info
@@ -72,7 +79,7 @@
 def prep(keys, values, docs, size):
     _, rows, width = keys.shape
     cols = width // size
-    own = jax.ShapeDtypeStruct((size, 2 * rows, cols), keys.dtype)
+    own = jax.ShapeDtypeStruct((size, 2 * rows + INFO, cols), keys.dtype)
     onward = jax.ShapeDtypeStruct((2 * rows + INFO, cols), keys.dtype)
 
     def kernel(*refs):
@@ -87,9 +94,17 @@
     )(keys, values, docs)
 
 
-def own_kernel(q_ref, kv_ref, docs_ref, o_ref, l_ref, k_ref, vx_ref, bias_ref, first_ref):
+def row_of_docs(kv_ref, tok):
+    cols = kv_ref.shape[2]
+    table = kv_ref[0, kv_ref.shape[1] - INFO :, :].astype(jnp.float32)
+    return jnp.concatenate([table[i : i + 1] for i in range(tok // cols)], axis=1)
+
+
+def own_kernel(q_ref, kv_ref, o_ref, l_ref, k_ref, vx_ref, bias_ref, docs_ref, first_ref):
     turn = pl.program_id(1)
-    parts, rows = kv_ref.shape[0], kv_ref.shape[1] // 2
+    parts, rows = kv_ref.shape[0], (kv_ref.shape[1] - INFO) // 2
+    group = pl.program_id(0)
+    lanes = pl.ds(pl.multiple_of(group * HEAD, HEAD), HEAD)
     tok = parts * rows
     turns = tok // BLOCK
     share = q_ref.shape[1] // HEAD
@@ -97,13 +112,14 @@
     @pl.when(turn == 0)
     def _():
         for j in range(parts):
-            k_ref[j * rows : (j + 1) * rows] = kv_ref[j, :rows]
-            vx_ref[j * rows : (j + 1) * rows, :HEAD] = kv_ref[j, rows:]
+            k_ref[j * rows : (j + 1) * rows] = kv_ref[j, :rows, lanes]
+            vx_ref[j * rows : (j + 1) * rows, :HEAD] = kv_ref[j, rows : 2 * rows, lanes]
             vx_ref[j * rows : (j + 1) * rows, HEAD:] = jnp.ones((rows, HEAD), vx_ref.dtype)
 
-    @pl.when((turn == 0) & (pl.program_id(0) == 0))
+    @pl.when((turn == 0) & (group == 0))
     def _():
-        docs = docs_ref[...]
+        docs = row_of_docs(kv_ref, tok)
+        docs_ref[...] = docs
         for t in range(turns):
             first_ref[t] = count(docs < docs[:, t * BLOCK : t * BLOCK + 1]) // BLOCK
 
@@ -133,9 +149,9 @@
                 l_ref[h : h + 1, :] = eye_rows(jnp.log2(total))
 
 
-def own_part(queries, kv, docs):
+def own_part(queries, kv):
     tok, width = queries.shape
-    parts, twice, cols = kv.shape
+    parts, longer, cols = kv.shape
     groups = cols // HEAD
     turns = tok // BLOCK
     share = width // HEAD // groups
@@ -144,8 +160,7 @@
         grid=(groups, turns),
         in_specs=[
             pl.BlockSpec((BLOCK, share * HEAD), lambda g, t: (t, g)),
-            pl.BlockSpec((parts, twice, HEAD), lambda g, t: (0, 0, g)),
-            pl.BlockSpec((1, tok), lambda g, t: (0, 0)),
+            pl.BlockSpec((parts, longer, cols), lambda g, t: (0, 0, 0)),
         ],
         out_specs=(
             pl.BlockSpec((BLOCK, share * HEAD), lambda g, t: (t, g)),
@@ -159,23 +174,24 @@
             pltpu.VMEM((tok, HEAD), jnp.bfloat16),
             pltpu.VMEM((tok, 2 * HEAD), jnp.bfloat16),
             pltpu.VMEM((BLOCK, tok), jnp.float32),
+            pltpu.VMEM((1, tok), jnp.float32),
             pltpu.SMEM((turns,), jnp.int32),
         ],
         compiler_params=pltpu.CompilerParams(vmem_limit_bytes=VMEM_LIMIT),
         cost_estimate=pl.CostEstimate(
             flops=4 * tok * tok * width, bytes_accessed=4 * tok * width, transcendentals=tok * tok * width // HEAD // 2
         ),
-    )(queries, kv, docs)
+    )(queries, kv)
 
 
 def beyond(logs):
     return jnp.logical_not((logs > -FLOOR) & (logs < CEILING))
 
 
-def rest_kernel(size, owner_ref, q_hbm, lown_ref, docs_ref, kv_ref, *refs):
+def rest_kernel(size, owner_ref, q_hbm, lown_ref, kv_ref, *refs):
     old_refs = refs[:size]
     done_hbm, o_hbm, send_ref, q_ref, o_ref, k_ref, vx_ref, new_ref, l_ref, acc_ref, top_ref = refs[size : size + 11]
-    q_sem, d_sem, o_sem = refs[size + 11 :]
+    docs_ref, q_sem, d_sem, o_sem = refs[size + 11 :]
     del done_hbm
     turns = q_ref.shape[0]
     groups = vx_ref.shape[0]
@@ -185,8 +201,8 @@
     tok = turns * BLOCK
 
     info = old_refs[0][2 * rows :, :HEAD].astype(jnp.float32)
-    docs = docs_ref[...]
-    same = info[0:1] == docs[:, :1].astype(jnp.float32)
+    docs = row_of_docs(kv_ref, tok)
+    same = info[0:1] == docs[:, :1]
     ahead = jnp.max(jnp.where(same, info[1:2] * CODE + info[2:3], 0.0)).astype(jnp.int32)
     behind = count(docs == docs[:, :1])
     steps = jnp.where(ahead > 0, (behind + BLOCK - 1) // BLOCK, 0)
@@ -210,7 +226,7 @@
     new_ref[...] = jnp.zeros(new_ref.shape, jnp.float32)
     here = lax.axis_index("head")
     for m in range(size):
-        base = pl.multiple_of(lax.rem(here + size - m, size) * rows, rows)
+        base = pl.multiple_of(jnp.bitwise_xor(here, m) * rows, rows)
         for g in range(groups):
             lanes = slice(g * HEAD, (g + 1) * HEAD)
             k_ref[g, pl.ds(base, rows), :] = old_refs[m][:rows, lanes]
@@ -221,12 +237,13 @@
         q_copy(turn).wait()
         d_copy(turn).wait()
         start = pl.multiple_of(turn * BLOCK, BLOCK)
-        inside = start + lax.broadcasted_iota(jnp.int32, (BLOCK, HEAD), 0) < behind
-        for n in range(1, turns + 1):
-
-            @pl.when((ahead + BLOCK - 1) // BLOCK == n)
-            def _(n=n):
+        short = behind - start <= BLOCK // 2
+        for n, tall in itertools.product(range(1, turns + 1), (BLOCK // 2, BLOCK)):
+
+            @pl.when(((ahead + BLOCK - 1) // BLOCK == n) & (short == (tall < BLOCK)))
+            def _(n=n, tall=tall):
                 width = n * BLOCK
+                inside = start + lax.broadcasted_iota(jnp.int32, (tall, HEAD), 0) < behind
                 place = lax.broadcasted_iota(jnp.int32, (1, width), 1)
                 bias = jnp.where(place >= width - ahead, 0.0, NEG)
 
@@ -234,19 +251,19 @@
                     k = k_ref[g, tok - width :, :]
                     vx = vx_ref[g, tok - width :, :]
                     top_head = pl.multiple_of(g * share, share)
-                    weights = jnp.exp2(lown_ref[pl.ds(top_head, share), pl.ds(start, BLOCK)])
+                    weights = jnp.exp2(lown_ref[pl.ds(top_head, share), pl.ds(start, tall)])
                     found = []
                     for h in range(share):
                         lanes = pl.ds(pl.multiple_of((g * share + h) * HEAD, HEAD), HEAD)
-                        s = f32_dot(q_ref[turn, :, lanes], k, NT) * SCALE2 + bias
+                        s = f32_dot(q_ref[turn, :tall, lanes], k, NT) * SCALE2 + bias
                         got = f32_dot(jnp.exp2(s).astype(jnp.bfloat16), vx, NN)
                         total = jnp.where(inside, got[:, HEAD:], 0.0)
-                        before = o_ref[turn, :, lanes].astype(jnp.float32)
+                        before = o_ref[turn, :tall, lanes].astype(jnp.float32)
                         weight = row_column(weights[h : h + 1])
                         mixed = (before * weight + got[:, :HEAD]) / (weight + total)
-                        o_ref[turn, :, lanes] = jnp.where(inside, mixed, before).astype(o_ref.dtype)
+                        o_ref[turn, :tall, lanes] = jnp.where(inside, mixed, before).astype(o_ref.dtype)
                         found.append(eye_rows(total))
-                    new_ref[pl.ds(top_head, share), pl.ds(start, BLOCK)] = jnp.concatenate(found, axis=0)
+                    new_ref[pl.ds(top_head, share), pl.ds(start, tall)] = jnp.concatenate(found, axis=0)
                     return 0
 
                 lax.fori_loop(0, groups, one_group, 0)
@@ -269,6 +286,8 @@
 
     @pl.when(bad > 0)
     def _():
+        docs_ref[...] = docs
+
         def every(turn, _):
             q_copy(turn).start()
             q_copy(turn).wait()
@@ -309,7 +328,7 @@
                     per = BLOCK // rows
                     group = pl.ds(pl.multiple_of(g * HEAD, HEAD), HEAD)
                     k = jnp.concatenate([kv_ref[j * per + i, :rows, group] for i in range(per)], axis=0)
-                    v = jnp.concatenate([kv_ref[j * per + i, rows:, group] for i in range(per)], axis=0)
+                    v = jnp.concatenate([kv_ref[j * per + i, rows : 2 * rows, group] for i in range(per)], axis=0)
                     add(keep, k, v)
                     return 0
 
@@ -335,7 +354,7 @@
         send_ref[o] = found
 
 
-def rest_part(owner, queries, lown, docs, kv, old, done, owners, piece):
+def rest_part(owner, queries, lown, kv, old, done, owners, piece):
     tok, width = queries.shape
     size = len(old)
     heads = width // HEAD
@@ -347,13 +366,13 @@
 
     return pl.pallas_call(
         kernel,
-        in_specs=[IN_SMEM, IN_HBM, IN_VMEM, IN_VMEM, IN_VMEM] + [IN_VMEM] * size + [IN_HBM],
+        in_specs=[IN_SMEM, IN_HBM, IN_VMEM, IN_VMEM] + [IN_VMEM] * size + [IN_HBM],
         out_specs=(IN_HBM, IN_VMEM),
         out_shape=(
             jax.ShapeDtypeStruct((tok, width), jnp.bfloat16),
             jax.ShapeDtypeStruct((owners, heads, piece), jnp.float32),
         ),
-        input_output_aliases={5 + size: 0},
+        input_output_aliases={4 + size: 0},
         scratch_shapes=[
             pltpu.VMEM((turns, BLOCK, width), jnp.bfloat16),
             pltpu.VMEM((turns, BLOCK, width), jnp.bfloat16),
@@ -363,6 +382,7 @@
             pltpu.VMEM((heads, tok), jnp.float32),
             pltpu.VMEM((BLOCK, 2 * HEAD), jnp.float32),
             pltpu.VMEM((BLOCK, HEAD), jnp.float32),
+            pltpu.VMEM((1, tok), jnp.float32),
             pltpu.SemaphoreType.DMA((turns,)),
             pltpu.SemaphoreType.DMA((turns,)),
             pltpu.SemaphoreType.DMA((turns,)),
@@ -371,7 +391,7 @@
         cost_estimate=pl.CostEstimate(
             flops=tok * tok * width, bytes_accessed=4 * tok * width, transcendentals=tok * tok * heads // 4
         ),
-    )(owner, queries, lown, docs, kv, *old, done)
+    )(owner, queries, lown, kv, *old, done)
 
 
 def spread_kernel(x_ref, o_ref):
@@ -393,21 +413,20 @@
     ctx_size, head_size = lax.axis_size("ctx"), lax.axis_size("head")
     tok, _ = queries.shape
     piece = 2 * tok // ctx_size
-    docs = doc_ids.reshape(1, tok)
-
-    own_send, *next_send = prep(keys, values, docs, head_size)
+
+    own_send, *next_send = prep(keys, values, doc_ids.reshape(1, tok), head_size)
     kv = lax.all_to_all(own_send, "head", 0, 0, tiled=True)
     old = []
     for m in range(head_size):
         route = [
-            (h * ctx_size + i, (h + m) % head_size * ctx_size + i + 1)
+            (h * ctx_size + i, (h ^ m) * ctx_size + i + 1)
             for h in range(head_size)
             for i in range(ctx_size - 1)
         ]
         old.append(lax.ppermute(next_send[m], ("head", "ctx"), route))
 
-    done, lown = own_part(queries, kv, docs)
-    attended, send = rest_part(piece_owner, queries, lown, docs, kv, old, done, ctx_size, piece)
+    done, lown = own_part(queries, kv)
+    attended, send = rest_part(piece_owner, queries, lown, kv, old, done, ctx_size, piece)
     got = lax.all_to_all(send, "ctx", 0, 0, tiled=True)
     return attended, spread(got)
 

time: 288 us -> 288 us (level)
  Pallas kernels: 243 us -> 246 us
    pallas_call x1, Pallas kernels: 13.4 us -> 16.8 us  [own_part(): pl.pallas_call(own_kernel, grid=(groups, turns), in_specs=[pl.BlockSpec((...]
  transfers between devices with their start and end apart: 5 -> 5, of which waited for: 0 -> 1; matrix products, arithmetic and copies ran while one was open for 0% -> 0% of each run, Pallas kernels for 5% -> 6%
where the time goes in v1:
time: 288 us; the launch traced here: 287 us
  Pallas kernels  246 us (85%)
  blocking collectives  20.9 us (7%)
  starting transfers between devices  19 us (7%)
    pallas_call x1, Pallas kernels, rest_part(): pl.pallas_call(kernel, in_specs=[IN_SMEM, IN_HBM, IN_VMEM, IN_VMEM] + [IN...  225 us
    all_to_all x1, blocking collectives, per_device(): got = lax.all_to_all(send, 'ctx', 0, 0, tiled=True)  20.9 us
    pallas_call x1, Pallas kernels, own_part(): pl.pallas_call(own_kernel, grid=(groups, turns), in_specs=[pl.BlockSpec((...  16.8 us
    ppermute x4, starting transfers between devices, per_device(): old.append(lax.ppermute(next_send[m], ('head', 'ctx'), route))  14.8 us
  transfers between devices with their start and end apart: 5, of which 1 were waited for; matrix products, arithmetic and copies ran while one was open for 0% of the time, Pallas kernels for 6%

profile of v1, /device:TPU:0, one launch (start us, length us, event | category | flops | bytes accessed | tf_op | source)
XLA Modules:
  0.0 287.1 jit_solution(13366894304113948507)
XLA Ops:
  0.6 2.7 shard_map.68
  3.3 4.2 %all-to-all-start = ((bf16[4,528,256]{2,1,0:T(8,128)(2,1)}), bf16[4,528,256]{2,1,0:T(8,128)(2,1)S(1)}, u32[]{:S(2)}, u32[]{:S(2)}) async-start(bf16[4,528,256]{2,1,0:T(8,128)(2,1)} %get-tuple-element.11), calls=%async_computation | async-start | bytes 2162688 | tf_op jit(solution)/shard_map/all_to_all | solution.py:418
  7.6 4.2 %collective-permute-start = (bf16[528,256]{1,0:T(8,128)(2,1)}, bf16[528,256]{1,0:T(8,128)(2,1)S(1)}, u32[]{:S(2)}, u32[]{:S(2)}) collective-permute-start(bf16[528,256]{1,0:T(8,128)(2,1)} %get-tuple-element.13), channel_id=1, source_target_pairs={{0,1},{1,2},{2,3},{3,4},{4,5},{5,6},{6,7},{8,9},{9,10},{10,11},{11... | collective-permute-start | bytes 811016 | tf_op jit(solution)/shard_map/ppermute | solution.py:426
  11.7 3.2 %collective-permute-start.1 = (bf16[528,256]{1,0:T(8,128)(2,1)}, bf16[528,256]{1,0:T(8,128)(2,1)S(1)}, u32[]{:S(2)}, u32[]{:S(2)}) collective-permute-start(bf16[528,256]{1,0:T(8,128)(2,1)} %get-tuple-element.14), channel_id=1, source_target_pairs={{0,9},{1,10},{2,11},{3,12},{4,13},{5,14},{6,15},{8,1},{9,2},{10,3}... | collective-permute-start | bytes 811016 | tf_op jit(solution)/shard_map/ppermute | solution.py:426
  15.0 4.5 %collective-permute-start.2 = (bf16[528,256]{1,0:T(8,128)(2,1)}, bf16[528,256]{1,0:T(8,128)(2,1)S(1)}, u32[]{:S(2)}, u32[]{:S(2)}) collective-permute-start(bf16[528,256]{1,0:T(8,128)(2,1)} %get-tuple-element.15), channel_id=1, source_target_pairs={{0,17},{1,18},{2,19},{3,20},{4,21},{5,22},{6,23},{8,25},{9,26},{10... | collective-permute-start | bytes 811016 | tf_op jit(solution)/shard_map/ppermute | solution.py:426
  19.5 0.0 copy-start
  19.5 2.9 %collective-permute-start.3 = (bf16[528,256]{1,0:T(8,128)(2,1)}, bf16[528,256]{1,0:T(8,128)(2,1)S(1)}, u32[]{:S(2)}, u32[]{:S(2)}) collective-permute-start(bf16[528,256]{1,0:T(8,128)(2,1)} %get-tuple-element.16), channel_id=1, source_target_pairs={{0,25},{1,26},{2,27},{3,28},{4,29},{5,30},{6,31},{8,17},{9,18},{10... | collective-permute-start | bytes 811016 | tf_op jit(solution)/shard_map/ppermute | solution.py:426
  22.4 0.7 all-to-all-done.kv_ref.refs_3_
  23.1 16.8 %shard_map.69 = (bf16[1024,2048]{1,0:T(8,128)(2,1)}, f32[16,1024]{1,0:T(8,128)S(1)}) custom-call(bf16[1024,2048]{1,0:T(8,128)(2,1)} %refs_1_.3, bf16[4,528,256]{2,1,0:T(8,128)(2,1)S(1)} %all-to-all-done.kv_ref.refs_3_), custom_call_target="tpu_custom_call" | custom-call | flops 8589934592 | bytes 8388608 | tf_op jit(solution)/shard_map/pallas_call | solution.py:158
  39.8 0.0 collective-permute-done.refs_4_
  39.8 0.0 collective-permute-done.1.refs_5_
  39.8 0.0 collective-permute-done.2.refs_6_
  39.9 0.0 collective-permute-done.3.refs_7_
  39.9 0.0 copy-done
  39.9 224.7 %shard_map.70 = (bf16[1024,2048]{1,0:T(8,128)(2,1)}, f32[8,16,256]{2,1,0:T(8,128)S(1)}) custom-call(s32[4]{0:T(128)S(1)} %copy-done, bf16[1024,2048]{1,0:T(8,128)(2,1)} %refs_1_.3, f32[16,1024]{1,0:T(8,128)S(1)} %get-tuple-element.12.refs_2_, bf16[4,528,256]{2,1,0:T(8,128)(2,1)S(1)} %all-to-all-done.kv_ref.refs_3_, ...), custom_call_target="tpu_custom_call", output_to_operand_aliasing={{0}: (8, {})} | custom-call | flops 2147483648 | bytes 8388608 | tf_op jit(solution)/shard_map/pallas_call | solution.py:367
  264.6 20.9 %all_to_all.10.x_ref = f32[8,16,256]{2,1,0:T(8,128)} all-to-all(f32[8,16,256]{2,1,0:T(8,128)S(1)} %get-tuple-element.19), channel_id=1, replica_groups=mesh['head'=4,'ctx'=8] {'ctx'}, dimensions={0} | all-to-all | bytes 262144 | tf_op jit(solution)/shard_map/all_to_all | solution.py:430
  285.5 1.6 shard_map.71
Async XLA Ops:
  3.3 19.8 %all-to-all-start = ((bf16[4,528,256]{2,1,0:T(8,128)(2,1)}), bf16[4,528,256]{2,1,0:T(8,128)(2,1)S(1)}, u32[]{:S(2)}, u32[]{:S(2)}) async-start(bf16[4,528,256]{2,1,0:T(8,128)(2,1)} %get-tuple-element.11), calls=%async_computation | async-start | bytes 2162688 | tf_op jit(solution)/shard_map/all_to_all | solution.py:418
  7.6 32.3 %collective-permute-start = (bf16[528,256]{1,0:T(8,128)(2,1)}, bf16[528,256]{1,0:T(8,128)(2,1)S(1)}, u32[]{:S(2)}, u32[]{:S(2)}) collective-permute-start(bf16[528,256]{1,0:T(8,128)(2,1)} %get-tuple-element.13), channel_id=1, source_target_pairs={{0,1},{1,2},{2,3},{3,4},{4,5},{5,6},{6,7},{8,9},{9,10},{10,11},{11... | collective-permute-start | bytes 811016 | tf_op jit(solution)/shard_map/ppermute | solution.py:426
  11.7 28.1 %collective-permute-start.1 = (bf16[528,256]{1,0:T(8,128)(2,1)}, bf16[528,256]{1,0:T(8,128)(2,1)S(1)}, u32[]{:S(2)}, u32[]{:S(2)}) collective-permute-start(bf16[528,256]{1,0:T(8,128)(2,1)} %get-tuple-element.14), channel_id=1, source_target_pairs={{0,9},{1,10},{2,11},{3,12},{4,13},{5,14},{6,15},{8,1},{9,2},{10,3}... | collective-permute-start | bytes 811016 | tf_op jit(solution)/shard_map/ppermute | solution.py:426
  15.0 24.9 %collective-permute-start.2 = (bf16[528,256]{1,0:T(8,128)(2,1)}, bf16[528,256]{1,0:T(8,128)(2,1)S(1)}, u32[]{:S(2)}, u32[]{:S(2)}) collective-permute-start(bf16[528,256]{1,0:T(8,128)(2,1)} %get-tuple-element.15), channel_id=1, source_target_pairs={{0,17},{1,18},{2,19},{3,20},{4,21},{5,22},{6,23},{8,25},{9,26},{10... | collective-permute-start | bytes 811016 | tf_op jit(solution)/shard_map/ppermute | solution.py:426
  19.5 20.4 %copy-start = (s32[4]{0:T(128)S(1)}, s32[4]{0:T(128)}, u32[]{:S(2)}) copy-start(s32[4]{0:T(128)} %refs_0_.3) | copy-start | bytes 52
  19.5 20.3 %collective-permute-start.3 = (bf16[528,256]{1,0:T(8,128)(2,1)}, bf16[528,256]{1,0:T(8,128)(2,1)S(1)}, u32[]{:S(2)}, u32[]{:S(2)}) collective-permute-start(bf16[528,256]{1,0:T(8,128)(2,1)} %get-tuple-element.16), channel_id=1, source_target_pairs={{0,25},{1,26},{2,27},{3,28},{4,29},{5,30},{6,31},{8,17},{9,18},{10... | collective-permute-start | bytes 811016 | tf_op jit(solution)/shard_map/ppermute | solution.py:426

commit v2 on v1

--- a/solution.py
+++ b/solution.py
@@ -101,27 +101,25 @@
 
 
 def own_kernel(q_ref, kv_ref, o_ref, l_ref, k_ref, vx_ref, bias_ref, docs_ref, first_ref):
-    turn = pl.program_id(1)
+    turn = pl.program_id(0)
     parts, rows = kv_ref.shape[0], (kv_ref.shape[1] - INFO) // 2
-    group = pl.program_id(0)
-    lanes = pl.ds(pl.multiple_of(group * HEAD, HEAD), HEAD)
+    groups = vx_ref.shape[0]
     tok = parts * rows
     turns = tok // BLOCK
-    share = q_ref.shape[1] // HEAD
+    share = q_ref.shape[1] // HEAD // groups
 
     @pl.when(turn == 0)
-    def _():
-        for j in range(parts):
-            k_ref[j * rows : (j + 1) * rows] = kv_ref[j, :rows, lanes]
-            vx_ref[j * rows : (j + 1) * rows, :HEAD] = kv_ref[j, rows : 2 * rows, lanes]
-            vx_ref[j * rows : (j + 1) * rows, HEAD:] = jnp.ones((rows, HEAD), vx_ref.dtype)
-
-    @pl.when((turn == 0) & (group == 0))
     def _():
         docs = row_of_docs(kv_ref, tok)
         docs_ref[...] = docs
         for t in range(turns):
             first_ref[t] = count(docs < docs[:, t * BLOCK : t * BLOCK + 1]) // BLOCK
+        for j in range(parts):
+            span = slice(j * rows, (j + 1) * rows)
+            k_ref[span] = kv_ref[j, :rows]
+            for g in range(groups):
+                vx_ref[g, span, :HEAD] = kv_ref[j, rows : 2 * rows, g * HEAD : (g + 1) * HEAD]
+                vx_ref[g, span, HEAD:] = jnp.ones((rows, HEAD), vx_ref.dtype)
 
     first = first_ref[turn]
     for n in range(1, turns + 1):
@@ -138,12 +136,12 @@
             )
             keep = (jnp.concatenate([q_docs] * (width // HEAD), axis=1) == k_docs) & (ahead <= width - BLOCK)
             bias_ref[:, :width] = jnp.where(keep, 0.0, NEG)
-            k = k_ref[pl.ds(base, width), :]
-            vx = vx_ref[pl.ds(base, width), :]
-            for h in range(share):
+            for h in range(groups * share):
+                g = h // share
                 lanes = slice(h * HEAD, (h + 1) * HEAD)
+                k = k_ref[pl.ds(base, width), g * HEAD : (g + 1) * HEAD]
                 s = f32_dot(q_ref[:, lanes], k, NT) * SCALE2 + bias_ref[:, :width]
-                got = f32_dot(jnp.exp2(s).astype(jnp.bfloat16), vx, NN)
+                got = f32_dot(jnp.exp2(s).astype(jnp.bfloat16), vx_ref[g, pl.ds(base, width), :], NN)
                 total = got[:, HEAD:]
                 o_ref[:, lanes] = (got[:, :HEAD] / total).astype(o_ref.dtype)
                 l_ref[h : h + 1, :] = eye_rows(jnp.log2(total))
@@ -151,31 +149,28 @@
 
 def own_part(queries, kv):
     tok, width = queries.shape
-    parts, longer, cols = kv.shape
-    groups = cols // HEAD
-    turns = tok // BLOCK
-    share = width // HEAD // groups
+    groups = kv.shape[2] // HEAD
     return pl.pallas_call(
         own_kernel,
-        grid=(groups, turns),
+        grid=(tok // BLOCK,),
         in_specs=[
-            pl.BlockSpec((BLOCK, share * HEAD), lambda g, t: (t, g)),
-            pl.BlockSpec((parts, longer, cols), lambda g, t: (0, 0, 0)),
+            pl.BlockSpec((BLOCK, width), lambda t: (t, 0)),
+            pl.BlockSpec(kv.shape, lambda t: (0, 0, 0)),
         ],
         out_specs=(
-            pl.BlockSpec((BLOCK, share * HEAD), lambda g, t: (t, g)),
-            pl.BlockSpec((share, BLOCK), lambda g, t: (g, t)),
+            pl.BlockSpec((BLOCK, width), lambda t: (t, 0)),
+            pl.BlockSpec((width // HEAD, BLOCK), lambda t: (0, t)),
         ),
         out_shape=(
             jax.ShapeDtypeStruct((tok, width), jnp.bfloat16),
             jax.ShapeDtypeStruct((width // HEAD, tok), jnp.float32),
         ),
         scratch_shapes=[
-            pltpu.VMEM((tok, HEAD), jnp.bfloat16),
-            pltpu.VMEM((tok, 2 * HEAD), jnp.bfloat16),
+            pltpu.VMEM((tok, groups * HEAD), jnp.bfloat16),
+            pltpu.VMEM((groups, tok, 2 * HEAD), jnp.bfloat16),
             pltpu.VMEM((BLOCK, tok), jnp.float32),
             pltpu.VMEM((1, tok), jnp.float32),
-            pltpu.SMEM((turns,), jnp.int32),
+            pltpu.SMEM((tok // BLOCK,), jnp.int32),
         ],
         compiler_params=pltpu.CompilerParams(vmem_limit_bytes=VMEM_LIMIT),
         cost_estimate=pl.CostEstimate(
@@ -200,6 +195,17 @@
     rows = (old_refs[0].shape[0] - INFO) // 2
     tok = turns * BLOCK
 
+    def q_copy(turn):
+        return pltpu.make_async_copy(tile_of(q_hbm, turn), q_ref.at[turn], q_sem.at[turn])
+
+    def d_copy(turn):
+        return pltpu.make_async_copy(tile_of(o_hbm, turn), o_ref.at[turn], d_sem.at[turn])
+
+    def o_copy(turn):
+        return pltpu.make_async_copy(o_ref.at[turn], tile_of(o_hbm, turn), o_sem.at[turn])
+
+    q_copy(0).start()
+    d_copy(0).start()
     info = old_refs[0][2 * rows :, :HEAD].astype(jnp.float32)
     docs = row_of_docs(kv_ref, tok)
     same = info[0:1] == docs[:, :1]
@@ -207,16 +213,7 @@
     behind = count(docs == docs[:, :1])
     steps = jnp.where(ahead > 0, (behind + BLOCK - 1) // BLOCK, 0)
 
-    def q_copy(turn):
-        return pltpu.make_async_copy(tile_of(q_hbm, turn), q_ref.at[turn], q_sem.at[turn])
-
-    def d_copy(turn):
-        return pltpu.make_async_copy(tile_of(o_hbm, turn), o_ref.at[turn], d_sem.at[turn])
-
-    def o_copy(turn):
-        return pltpu.make_async_copy(o_ref.at[turn], tile_of(o_hbm, turn), o_sem.at[turn])
-
-    for turn in range(turns):
+    for turn in range(1, turns):
 
         @pl.when(turn < steps)
         def _(turn=turn):
@@ -272,6 +269,12 @@
         return 0
 
     lax.fori_loop(0, steps, one, 0)
+
+    @pl.when(steps == 0)
+    def _():
+        q_copy(0).wait()
+        d_copy(0).wait()
+
     own = lown_ref[...]
     new = new_ref[...]
     l_ref[...] = jnp.log2(jnp.exp2(own) + new)

time: 288 us -> 287 us (level)
  Pallas kernels: 246 us -> 242 us
    pallas_call x1, Pallas kernels: 16.8 us -> 11.9 us  [own_part(): pl.pallas_call(own_kernel, grid=(tok // BLOCK,), in_specs=[pl.BlockSpec((...]
  transfers between devices with their start and end apart: 5 -> 5, of which waited for: 1 -> 2; matrix products, arithmetic and copies ran while one was open for 0% -> 0% of each run, Pallas kernels for 6% -> 4%
where the time goes in v2:
time: 287 us; the launch traced here: 286 us
  Pallas kernels  242 us (84%)
  blocking collectives  23.4 us (8%)
  starting transfers between devices  19 us (7%)
    pallas_call x1, Pallas kernels, rest_part(): pl.pallas_call(kernel, in_specs=[IN_SMEM, IN_HBM, IN_VMEM, IN_VMEM] + [IN...  226 us
    all_to_all x1, blocking collectives, per_device(): got = lax.all_to_all(send, 'ctx', 0, 0, tiled=True)  23.4 us
    ppermute x4, starting transfers between devices, per_device(): old.append(lax.ppermute(next_send[m], ('head', 'ctx'), route))  14.8 us
    pallas_call x1, Pallas kernels, own_part(): pl.pallas_call(own_kernel, grid=(tok // BLOCK,), in_specs=[pl.BlockSpec((...  11.9 us
  transfers between devices with their start and end apart: 5, of which 2 were waited for; matrix products, arithmetic and copies ran while one was open for 0% of the time, Pallas kernels for 4%

profile of v2, /device:TPU:0, one launch (start us, length us, event | category | flops | bytes accessed | tf_op | source)
XLA Modules:
  0.0 286.4 jit_solution(9917239448772052782)
XLA Ops:
  0.6 2.7 shard_map.68
  3.3 4.2 %all-to-all-start = ((bf16[4,528,256]{2,1,0:T(8,128)(2,1)}), bf16[4,528,256]{2,1,0:T(8,128)(2,1)S(1)}, u32[]{:S(2)}, u32[]{:S(2)}) async-start(bf16[4,528,256]{2,1,0:T(8,128)(2,1)} %get-tuple-element.11), calls=%async_computation | async-start | bytes 2162688 | tf_op jit(solution)/shard_map/all_to_all | solution.py:421
  7.6 4.2 %collective-permute-start = (bf16[528,256]{1,0:T(8,128)(2,1)}, bf16[528,256]{1,0:T(8,128)(2,1)S(1)}, u32[]{:S(2)}, u32[]{:S(2)}) collective-permute-start(bf16[528,256]{1,0:T(8,128)(2,1)} %get-tuple-element.13), channel_id=1, source_target_pairs={{0,1},{1,2},{2,3},{3,4},{4,5},{5,6},{6,7},{8,9},{9,10},{10,11},{11... | collective-permute-start | bytes 811016 | tf_op jit(solution)/shard_map/ppermute | solution.py:429
  11.7 3.2 %collective-permute-start.1 = (bf16[528,256]{1,0:T(8,128)(2,1)}, bf16[528,256]{1,0:T(8,128)(2,1)S(1)}, u32[]{:S(2)}, u32[]{:S(2)}) collective-permute-start(bf16[528,256]{1,0:T(8,128)(2,1)} %get-tuple-element.14), channel_id=1, source_target_pairs={{0,9},{1,10},{2,11},{3,12},{4,13},{5,14},{6,15},{8,1},{9,2},{10,3}... | collective-permute-start | bytes 811016 | tf_op jit(solution)/shard_map/ppermute | solution.py:429
  15.0 4.5 %collective-permute-start.2 = (bf16[528,256]{1,0:T(8,128)(2,1)}, bf16[528,256]{1,0:T(8,128)(2,1)S(1)}, u32[]{:S(2)}, u32[]{:S(2)}) collective-permute-start(bf16[528,256]{1,0:T(8,128)(2,1)} %get-tuple-element.15), channel_id=1, source_target_pairs={{0,17},{1,18},{2,19},{3,20},{4,21},{5,22},{6,23},{8,25},{9,26},{10... | collective-permute-start | bytes 811016 | tf_op jit(solution)/shard_map/ppermute | solution.py:429
  19.5 0.0 copy-start
  19.5 2.9 %collective-permute-start.3 = (bf16[528,256]{1,0:T(8,128)(2,1)}, bf16[528,256]{1,0:T(8,128)(2,1)S(1)}, u32[]{:S(2)}, u32[]{:S(2)}) collective-permute-start(bf16[528,256]{1,0:T(8,128)(2,1)} %get-tuple-element.16), channel_id=1, source_target_pairs={{0,25},{1,26},{2,27},{3,28},{4,29},{5,30},{6,31},{8,17},{9,18},{10... | collective-permute-start | bytes 811016 | tf_op jit(solution)/shard_map/ppermute | solution.py:429
  22.4 0.7 all-to-all-done.kv_ref.refs_3_
  23.1 11.9 %shard_map.69 = (bf16[1024,2048]{1,0:T(8,128)(2,1)}, f32[16,1024]{1,0:T(8,128)S(1)}) custom-call(bf16[1024,2048]{1,0:T(8,128)(2,1)} %refs_1_.3, bf16[4,528,256]{2,1,0:T(8,128)(2,1)S(1)} %all-to-all-done.kv_ref.refs_3_), custom_call_target="tpu_custom_call" | custom-call | flops 8589934592 | bytes 8388608 | tf_op jit(solution)/shard_map/pallas_call | solution.py:153
  35.0 0.0 collective-permute-done.refs_4_
  35.0 0.8 collective-permute-done.1.refs_5_
  35.8 0.0 collective-permute-done.2.refs_6_
  35.8 0.0 collective-permute-done.3.refs_7_
  35.8 0.0 copy-done
  35.8 225.7 %shard_map.70 = (bf16[1024,2048]{1,0:T(8,128)(2,1)}, f32[8,16,256]{2,1,0:T(8,128)S(1)}) custom-call(s32[4]{0:T(128)S(1)} %copy-done, bf16[1024,2048]{1,0:T(8,128)(2,1)} %refs_1_.3, f32[16,1024]{1,0:T(8,128)S(1)} %get-tuple-element.12.refs_2_, bf16[4,528,256]{2,1,0:T(8,128)(2,1)S(1)} %all-to-all-done.kv_ref.refs_3_, ...), custom_call_target="tpu_custom_call", output_to_operand_aliasing={{0}: (8, {})} | custom-call | flops 2147483648 | bytes 8388608 | tf_op jit(solution)/shard_map/pallas_call | solution.py:370
  261.5 23.4 %all_to_all.10.x_ref = f32[8,16,256]{2,1,0:T(8,128)} all-to-all(f32[8,16,256]{2,1,0:T(8,128)S(1)} %get-tuple-element.19), channel_id=1, replica_groups=mesh['head'=4,'ctx'=8] {'ctx'}, dimensions={0} | all-to-all | bytes 262144 | tf_op jit(solution)/shard_map/all_to_all | solution.py:433
  284.9 1.6 shard_map.71
Async XLA Ops:
  3.3 19.8 %all-to-all-start = ((bf16[4,528,256]{2,1,0:T(8,128)(2,1)}), bf16[4,528,256]{2,1,0:T(8,128)(2,1)S(1)}, u32[]{:S(2)}, u32[]{:S(2)}) async-start(bf16[4,528,256]{2,1,0:T(8,128)(2,1)} %get-tuple-element.11), calls=%async_computation | async-start | bytes 2162688 | tf_op jit(solution)/shard_map/all_to_all | solution.py:421
  7.6 27.5 %collective-permute-start = (bf16[528,256]{1,0:T(8,128)(2,1)}, bf16[528,256]{1,0:T(8,128)(2,1)S(1)}, u32[]{:S(2)}, u32[]{:S(2)}) collective-permute-start(bf16[528,256]{1,0:T(8,128)(2,1)} %get-tuple-element.13), channel_id=1, source_target_pairs={{0,1},{1,2},{2,3},{3,4},{4,5},{5,6},{6,7},{8,9},{9,10},{10,11},{11... | collective-permute-start | bytes 811016 | tf_op jit(solution)/shard_map/ppermute | solution.py:429
  11.7 24.0 %collective-permute-start.1 = (bf16[528,256]{1,0:T(8,128)(2,1)}, bf16[528,256]{1,0:T(8,128)(2,1)S(1)}, u32[]{:S(2)}, u32[]{:S(2)}) collective-permute-start(bf16[528,256]{1,0:T(8,128)(2,1)} %get-tuple-element.14), channel_id=1, source_target_pairs={{0,9},{1,10},{2,11},{3,12},{4,13},{5,14},{6,15},{8,1},{9,2},{10,3}... | collective-permute-start | bytes 811016 | tf_op jit(solution)/shard_map/ppermute | solution.py:429
  15.0 20.8 %collective-permute-start.2 = (bf16[528,256]{1,0:T(8,128)(2,1)}, bf16[528,256]{1,0:T(8,128)(2,1)S(1)}, u32[]{:S(2)}, u32[]{:S(2)}) collective-permute-start(bf16[528,256]{1,0:T(8,128)(2,1)} %get-tuple-element.15), channel_id=1, source_target_pairs={{0,17},{1,18},{2,19},{3,20},{4,21},{5,22},{6,23},{8,25},{9,26},{10... | collective-permute-start | bytes 811016 | tf_op jit(solution)/shard_map/ppermute | solution.py:429
  19.5 16.3 %copy-start = (s32[4]{0:T(128)S(1)}, s32[4]{0:T(128)}, u32[]{:S(2)}) copy-start(s32[4]{0:T(128)} %refs_0_.3) | copy-start | bytes 52
  19.5 16.3 %collective-permute-start.3 = (bf16[528,256]{1,0:T(8,128)(2,1)}, bf16[528,256]{1,0:T(8,128)(2,1)S(1)}, u32[]{:S(2)}, u32[]{:S(2)}) collective-permute-start(bf16[528,256]{1,0:T(8,128)(2,1)} %get-tuple-element.16), channel_id=1, source_target_pairs={{0,25},{1,26},{2,27},{3,28},{4,29},{5,30},{6,31},{8,17},{9,18},{10... | collective-permute-start | bytes 811016 | tf_op jit(solution)/shard_map/ppermute | solution.py:429

commit v3 on v2

--- a/solution.py
+++ b/solution.py
@@ -244,14 +244,14 @@
                 place = lax.broadcasted_iota(jnp.int32, (1, width), 1)
                 bias = jnp.where(place >= width - ahead, 0.0, NEG)
 
-                def one_group(g, _):
+                for g in range(groups):
                     k = k_ref[g, tok - width :, :]
                     vx = vx_ref[g, tok - width :, :]
-                    top_head = pl.multiple_of(g * share, share)
+                    top_head = g * share
                     weights = jnp.exp2(lown_ref[pl.ds(top_head, share), pl.ds(start, tall)])
                     found = []
                     for h in range(share):
-                        lanes = pl.ds(pl.multiple_of((g * share + h) * HEAD, HEAD), HEAD)
+                        lanes = slice((g * share + h) * HEAD, (g * share + h + 1) * HEAD)
                         s = f32_dot(q_ref[turn, :tall, lanes], k, NT) * SCALE2 + bias
                         got = f32_dot(jnp.exp2(s).astype(jnp.bfloat16), vx, NN)
                         total = jnp.where(inside, got[:, HEAD:], 0.0)
@@ -261,9 +261,6 @@
                         o_ref[turn, :tall, lanes] = jnp.where(inside, mixed, before).astype(o_ref.dtype)
                         found.append(eye_rows(total))
                     new_ref[pl.ds(top_head, share), pl.ds(start, tall)] = jnp.concatenate(found, axis=0)
-                    return 0
-
-                lax.fori_loop(0, groups, one_group, 0)
 
         o_copy(turn).start()
         return 0

time: 287 us -> 283 us (0.986)
  blocking collectives: 23.4 us -> 19.8 us
    all_to_all x1, blocking collectives: 23.4 us -> 19.8 us  [per_device(): got = lax.all_to_all(send, 'ctx', 0, 0, tiled=True)]
where the time goes in v3:
time: 283 us
  Pallas kernels  242 us (86%)
  blocking collectives  19.8 us (7%)
  starting transfers between devices  19 us (7%)
    pallas_call x1, Pallas kernels, rest_part(): pl.pallas_call(kernel, in_specs=[IN_SMEM, IN_HBM, IN_VMEM, IN_VMEM] + [IN...  226 us
    all_to_all x1, blocking collectives, per_device(): got = lax.all_to_all(send, 'ctx', 0, 0, tiled=True)  19.8 us
    ppermute x4, starting transfers between devices, per_device(): old.append(lax.ppermute(next_send[m], ('head', 'ctx'), route))  14.8 us
    pallas_call x1, Pallas kernels, own_part(): pl.pallas_call(own_kernel, grid=(tok // BLOCK,), in_specs=[pl.BlockSpec((...  11.9 us
  transfers between devices with their start and end apart: 5, of which 2 were waited for; matrix products, arithmetic and copies ran while one was open for 0% of the time, Pallas kernels for 4%

profile of v3, /device:TPU:0, one launch (start us, length us, event | category | flops | bytes accessed | tf_op | source)
XLA Modules:
  0.0 282.9 jit_solution(8369564443950459985)
XLA Ops:
  0.6 2.7 shard_map.68
  3.3 4.2 %all-to-all-start = ((bf16[4,528,256]{2,1,0:T(8,128)(2,1)}), bf16[4,528,256]{2,1,0:T(8,128)(2,1)S(1)}, u32[]{:S(2)}, u32[]{:S(2)}) async-start(bf16[4,528,256]{2,1,0:T(8,128)(2,1)} %get-tuple-element.11), calls=%async_computation | async-start | bytes 2162688 | tf_op jit(solution)/shard_map/all_to_all | solution.py:418
  7.6 4.2 %collective-permute-start = (bf16[528,256]{1,0:T(8,128)(2,1)}, bf16[528,256]{1,0:T(8,128)(2,1)S(1)}, u32[]{:S(2)}, u32[]{:S(2)}) collective-permute-start(bf16[528,256]{1,0:T(8,128)(2,1)} %get-tuple-element.13), channel_id=1, source_target_pairs={{0,1},{1,2},{2,3},{3,4},{4,5},{5,6},{6,7},{8,9},{9,10},{10,11},{11... | collective-permute-start | bytes 811016 | tf_op jit(solution)/shard_map/ppermute | solution.py:426
  11.7 3.2 %collective-permute-start.1 = (bf16[528,256]{1,0:T(8,128)(2,1)}, bf16[528,256]{1,0:T(8,128)(2,1)S(1)}, u32[]{:S(2)}, u32[]{:S(2)}) collective-permute-start(bf16[528,256]{1,0:T(8,128)(2,1)} %get-tuple-element.14), channel_id=1, source_target_pairs={{0,9},{1,10},{2,11},{3,12},{4,13},{5,14},{6,15},{8,1},{9,2},{10,3}... | collective-permute-start | bytes 811016 | tf_op jit(solution)/shard_map/ppermute | solution.py:426
  15.0 4.5 %collective-permute-start.2 = (bf16[528,256]{1,0:T(8,128)(2,1)}, bf16[528,256]{1,0:T(8,128)(2,1)S(1)}, u32[]{:S(2)}, u32[]{:S(2)}) collective-permute-start(bf16[528,256]{1,0:T(8,128)(2,1)} %get-tuple-element.15), channel_id=1, source_target_pairs={{0,17},{1,18},{2,19},{3,20},{4,21},{5,22},{6,23},{8,25},{9,26},{10... | collective-permute-start | bytes 811016 | tf_op jit(solution)/shard_map/ppermute | solution.py:426
  19.5 0.0 copy-start
  19.5 2.9 %collective-permute-start.3 = (bf16[528,256]{1,0:T(8,128)(2,1)}, bf16[528,256]{1,0:T(8,128)(2,1)S(1)}, u32[]{:S(2)}, u32[]{:S(2)}) collective-permute-start(bf16[528,256]{1,0:T(8,128)(2,1)} %get-tuple-element.16), channel_id=1, source_target_pairs={{0,25},{1,26},{2,27},{3,28},{4,29},{5,30},{6,31},{8,17},{9,18},{10... | collective-permute-start | bytes 811016 | tf_op jit(solution)/shard_map/ppermute | solution.py:426
  22.4 0.7 all-to-all-done.kv_ref.refs_3_
  23.1 11.9 %shard_map.69 = (bf16[1024,2048]{1,0:T(8,128)(2,1)}, f32[16,1024]{1,0:T(8,128)S(1)}) custom-call(bf16[1024,2048]{1,0:T(8,128)(2,1)} %refs_1_.3, bf16[4,528,256]{2,1,0:T(8,128)(2,1)S(1)} %all-to-all-done.kv_ref.refs_3_), custom_call_target="tpu_custom_call" | custom-call | flops 8589934592 | bytes 8388608 | tf_op jit(solution)/shard_map/pallas_call | solution.py:153
  35.0 0.0 collective-permute-done.refs_4_
  35.0 0.8 collective-permute-done.1.refs_5_
  35.8 0.0 collective-permute-done.2.refs_6_
  35.8 0.0 collective-permute-done.3.refs_7_
  35.8 0.0 copy-done
  35.8 225.8 %shard_map.70 = (bf16[1024,2048]{1,0:T(8,128)(2,1)}, f32[8,16,256]{2,1,0:T(8,128)S(1)}) custom-call(s32[4]{0:T(128)S(1)} %copy-done, bf16[1024,2048]{1,0:T(8,128)(2,1)} %refs_1_.3, f32[16,1024]{1,0:T(8,128)S(1)} %get-tuple-element.12.refs_2_, bf16[4,528,256]{2,1,0:T(8,128)(2,1)S(1)} %all-to-all-done.kv_ref.refs_3_, ...), custom_call_target="tpu_custom_call", output_to_operand_aliasing={{0}: (8, {})} | custom-call | flops 2147483648 | bytes 8388608 | tf_op jit(solution)/shard_map/pallas_call | solution.py:367
  261.6 19.8 %all_to_all.10.x_ref = f32[8,16,256]{2,1,0:T(8,128)} all-to-all(f32[8,16,256]{2,1,0:T(8,128)S(1)} %get-tuple-element.19), channel_id=1, replica_groups=mesh['head'=4,'ctx'=8] {'ctx'}, dimensions={0} | all-to-all | bytes 262144 | tf_op jit(solution)/shard_map/all_to_all | solution.py:430
  281.3 1.6 shard_map.71
Async XLA Ops:
  3.3 19.8 %all-to-all-start = ((bf16[4,528,256]{2,1,0:T(8,128)(2,1)}), bf16[4,528,256]{2,1,0:T(8,128)(2,1)S(1)}, u32[]{:S(2)}, u32[]{:S(2)}) async-start(bf16[4,528,256]{2,1,0:T(8,128)(2,1)} %get-tuple-element.11), calls=%async_computation | async-start | bytes 2162688 | tf_op jit(solution)/shard_map/all_to_all | solution.py:418
  7.6 27.5 %collective-permute-start = (bf16[528,256]{1,0:T(8,128)(2,1)}, bf16[528,256]{1,0:T(8,128)(2,1)S(1)}, u32[]{:S(2)}, u32[]{:S(2)}) collective-permute-start(bf16[528,256]{1,0:T(8,128)(2,1)} %get-tuple-element.13), channel_id=1, source_target_pairs={{0,1},{1,2},{2,3},{3,4},{4,5},{5,6},{6,7},{8,9},{9,10},{10,11},{11... | collective-permute-start | bytes 811016 | tf_op jit(solution)/shard_map/ppermute | solution.py:426
  11.7 24.0 %collective-permute-start.1 = (bf16[528,256]{1,0:T(8,128)(2,1)}, bf16[528,256]{1,0:T(8,128)(2,1)S(1)}, u32[]{:S(2)}, u32[]{:S(2)}) collective-permute-start(bf16[528,256]{1,0:T(8,128)(2,1)} %get-tuple-element.14), channel_id=1, source_target_pairs={{0,9},{1,10},{2,11},{3,12},{4,13},{5,14},{6,15},{8,1},{9,2},{10,3}... | collective-permute-start | bytes 811016 | tf_op jit(solution)/shard_map/ppermute | solution.py:426
  15.0 20.8 %collective-permute-start.2 = (bf16[528,256]{1,0:T(8,128)(2,1)}, bf16[528,256]{1,0:T(8,128)(2,1)S(1)}, u32[]{:S(2)}, u32[]{:S(2)}) collective-permute-start(bf16[528,256]{1,0:T(8,128)(2,1)} %get-tuple-element.15), channel_id=1, source_target_pairs={{0,17},{1,18},{2,19},{3,20},{4,21},{5,22},{6,23},{8,25},{9,26},{10... | collective-permute-start | bytes 811016 | tf_op jit(solution)/shard_map/ppermute | solution.py:426
  19.5 16.3 %copy-start = (s32[4]{0:T(128)S(1)}, s32[4]{0:T(128)}, u32[]{:S(2)}) copy-start(s32[4]{0:T(128)} %refs_0_.3) | copy-start | bytes 52
  19.5 16.3 %collective-permute-start.3 = (bf16[528,256]{1,0:T(8,128)(2,1)}, bf16[528,256]{1,0:T(8,128)(2,1)S(1)}, u32[]{:S(2)}, u32[]{:S(2)}) collective-permute-start(bf16[528,256]{1,0:T(8,128)(2,1)} %get-tuple-element.16), channel_id=1, source_target_pairs={{0,25},{1,26},{2,27},{3,28},{4,29},{5,30},{6,31},{8,17},{9,18},{10... | collective-permute-start | bytes 811016 | tf_op jit(solution)/shard_map/ppermute | solution.py:426

commit v4 on v3

--- a/solution.py
+++ b/solution.py
@@ -131,11 +131,13 @@
             here = pl.multiple_of(turn * BLOCK, BLOCK)
             q_docs = row_column(docs_ref[:, pl.ds(here, BLOCK)])
             k_docs = docs_ref[:, pl.ds(base, width)]
-            ahead = lax.broadcasted_iota(jnp.int32, (BLOCK, width), 1) - lax.broadcasted_iota(
-                jnp.int32, (BLOCK, width), 0
+            keep = jnp.concatenate([q_docs] * (width // HEAD), axis=1) == k_docs
+            past = lax.broadcasted_iota(jnp.int32, (BLOCK, BLOCK), 1) <= lax.broadcasted_iota(
+                jnp.int32, (BLOCK, BLOCK), 0
             )
-            keep = (jnp.concatenate([q_docs] * (width // HEAD), axis=1) == k_docs) & (ahead <= width - BLOCK)
-            bias_ref[:, :width] = jnp.where(keep, 0.0, NEG)
+            if n > 1:
+                bias_ref[:, : width - BLOCK] = jnp.where(keep[:, : width - BLOCK], 0.0, NEG)
+            bias_ref[:, width - BLOCK : width] = jnp.where(keep[:, width - BLOCK :] & past, 0.0, NEG)
             for h in range(groups * share):
                 g = h // share
                 lanes = slice(h * HEAD, (h + 1) * HEAD)
@@ -155,7 +157,7 @@
         grid=(tok // BLOCK,),
         in_specs=[
             pl.BlockSpec((BLOCK, width), lambda t: (t, 0)),
-            pl.BlockSpec(kv.shape, lambda t: (0, 0, 0)),
+            IN_VMEM,
         ],
         out_specs=(
             pl.BlockSpec((BLOCK, width), lambda t: (t, 0)),
@@ -278,14 +280,16 @@
     token = lax.broadcasted_iota(jnp.int32, (heads, tok), 1)
     met = (token < behind) & (ahead > 0)
     bad = count(beyond(own) | (met & beyond(jnp.log2(new))))
-    for turn in range(turns):
-
-        @pl.when(turn < steps)
-        def _(turn=turn):
-            o_copy(turn).wait()
+    def wait_for_rows():
+        for turn in range(turns):
+
+            @pl.when(turn < steps)
+            def _(turn=turn):
+                o_copy(turn).wait()
 
     @pl.when(bad > 0)
     def _():
+        wait_for_rows()
         docs_ref[...] = docs
 
         def every(turn, _):
@@ -352,6 +356,10 @@
         for j in range(tok // piece):
             found = jnp.where(owner_ref[j] == o, l_ref[:, j * piece : (j + 1) * piece] * LN2, found)
         send_ref[o] = found
+
+    @pl.when(bad == 0)
+    def _():
+        wait_for_rows()
 
 
 def rest_part(owner, queries, lown, kv, old, done, owners, piece):

time: 283 us -> 286 us (1.011)
  Pallas kernels: 242 us -> 245 us
    pallas_call x1, Pallas kernels: 11.9 us -> 15.4 us  [own_part(): pl.pallas_call(own_kernel, grid=(tok // BLOCK,), in_specs=[pl.BlockSpec((...]
  transfers between devices with their start and end apart: 5 -> 5, of which waited for: 2 -> 1; matrix products, arithmetic and copies ran while one was open for 0% -> 0% of each run, Pallas kernels for 4% -> 5%
where the time goes in v4:
time: 286 us
  Pallas kernels  245 us (86%)
  blocking collectives  20.6 us (7%)
  starting transfers between devices  19 us (7%)
    pallas_call x1, Pallas kernels, rest_part(): pl.pallas_call(kernel, in_specs=[IN_SMEM, IN_HBM, IN_VMEM, IN_VMEM] + [IN...  226 us
    all_to_all x1, blocking collectives, per_device(): got = lax.all_to_all(send, 'ctx', 0, 0, tiled=True)  20.6 us
    pallas_call x1, Pallas kernels, own_part(): pl.pallas_call(own_kernel, grid=(tok // BLOCK,), in_specs=[pl.BlockSpec((...  15.4 us
    ppermute x4, starting transfers between devices, per_device(): old.append(lax.ppermute(next_send[m], ('head', 'ctx'), route))  14.8 us
  transfers between devices with their start and end apart: 5, of which 1 were waited for; matrix products, arithmetic and copies ran while one was open for 0% of the time, Pallas kernels for 5%

profile of v4, /device:TPU:0, one launch (start us, length us, event | category | flops | bytes accessed | tf_op | source)
XLA Modules:
  0.0 286.5 jit_solution(2290734273011544636)
XLA Ops:
  0.6 2.7 shard_map.68
  3.3 4.2 %all-to-all-start = ((bf16[4,528,256]{2,1,0:T(8,128)(2,1)}), bf16[4,528,256]{2,1,0:T(8,128)(2,1)S(1)}, u32[]{:S(2)}, u32[]{:S(2)}) async-start(bf16[4,528,256]{2,1,0:T(8,128)(2,1)} %get-tuple-element.11), calls=%async_computation | async-start | bytes 2162688 | tf_op jit(solution)/shard_map/all_to_all | solution.py:426
  7.6 4.2 %collective-permute-start = (bf16[528,256]{1,0:T(8,128)(2,1)}, bf16[528,256]{1,0:T(8,128)(2,1)S(1)}, u32[]{:S(2)}, u32[]{:S(2)}) collective-permute-start(bf16[528,256]{1,0:T(8,128)(2,1)} %get-tuple-element.13), channel_id=1, source_target_pairs={{0,1},{1,2},{2,3},{3,4},{4,5},{5,6},{6,7},{8,9},{9,10},{10,11},{11... | collective-permute-start | bytes 811016 | tf_op jit(solution)/shard_map/ppermute | solution.py:434
  11.7 3.2 %collective-permute-start.1 = (bf16[528,256]{1,0:T(8,128)(2,1)}, bf16[528,256]{1,0:T(8,128)(2,1)S(1)}, u32[]{:S(2)}, u32[]{:S(2)}) collective-permute-start(bf16[528,256]{1,0:T(8,128)(2,1)} %get-tuple-element.14), channel_id=1, source_target_pairs={{0,9},{1,10},{2,11},{3,12},{4,13},{5,14},{6,15},{8,1},{9,2},{10,3}... | collective-permute-start | bytes 811016 | tf_op jit(solution)/shard_map/ppermute | solution.py:434
  15.0 4.5 %collective-permute-start.2 = (bf16[528,256]{1,0:T(8,128)(2,1)}, bf16[528,256]{1,0:T(8,128)(2,1)S(1)}, u32[]{:S(2)}, u32[]{:S(2)}) collective-permute-start(bf16[528,256]{1,0:T(8,128)(2,1)} %get-tuple-element.15), channel_id=1, source_target_pairs={{0,17},{1,18},{2,19},{3,20},{4,21},{5,22},{6,23},{8,25},{9,26},{10... | collective-permute-start | bytes 811016 | tf_op jit(solution)/shard_map/ppermute | solution.py:434
  19.5 0.0 copy-start
  19.5 2.9 %collective-permute-start.3 = (bf16[528,256]{1,0:T(8,128)(2,1)}, bf16[528,256]{1,0:T(8,128)(2,1)S(1)}, u32[]{:S(2)}, u32[]{:S(2)}) collective-permute-start(bf16[528,256]{1,0:T(8,128)(2,1)} %get-tuple-element.16), channel_id=1, source_target_pairs={{0,25},{1,26},{2,27},{3,28},{4,29},{5,30},{6,31},{8,17},{9,18},{10... | collective-permute-start | bytes 811016 | tf_op jit(solution)/shard_map/ppermute | solution.py:434
  22.4 0.7 all-to-all-done.kv_ref.refs_3_
  23.1 15.4 %shard_map.69 = (bf16[1024,2048]{1,0:T(8,128)(2,1)}, f32[16,1024]{1,0:T(8,128)S(1)}) custom-call(bf16[1024,2048]{1,0:T(8,128)(2,1)} %refs_1_.3, bf16[4,528,256]{2,1,0:T(8,128)(2,1)S(1)} %all-to-all-done.kv_ref.refs_3_), custom_call_target="tpu_custom_call" | custom-call | flops 8589934592 | bytes 8388608 | tf_op jit(solution)/shard_map/pallas_call | solution.py:155
  38.5 0.0 collective-permute-done.refs_4_
  38.5 0.0 collective-permute-done.1.refs_5_
  38.5 0.0 collective-permute-done.2.refs_6_
  38.5 0.0 collective-permute-done.3.refs_7_
  38.5 0.0 copy-done
  38.5 225.8 %shard_map.70 = (bf16[1024,2048]{1,0:T(8,128)(2,1)}, f32[8,16,256]{2,1,0:T(8,128)S(1)}) custom-call(s32[4]{0:T(128)S(1)} %copy-done, bf16[1024,2048]{1,0:T(8,128)(2,1)} %refs_1_.3, f32[16,1024]{1,0:T(8,128)S(1)} %get-tuple-element.12.refs_2_, bf16[4,528,256]{2,1,0:T(8,128)(2,1)S(1)} %all-to-all-done.kv_ref.refs_3_, ...), custom_call_target="tpu_custom_call", output_to_operand_aliasing={{0}: (8, {})} | custom-call | flops 2147483648 | bytes 8388608 | tf_op jit(solution)/shard_map/pallas_call | solution.py:375
  264.3 20.6 %all_to_all.10.x_ref = f32[8,16,256]{2,1,0:T(8,128)} all-to-all(f32[8,16,256]{2,1,0:T(8,128)S(1)} %get-tuple-element.19), channel_id=1, replica_groups=mesh['head'=4,'ctx'=8] {'ctx'}, dimensions={0} | all-to-all | bytes 262144 | tf_op jit(solution)/shard_map/all_to_all | solution.py:438
  284.9 1.6 shard_map.71
Async XLA Ops:
  3.3 19.8 %all-to-all-start = ((bf16[4,528,256]{2,1,0:T(8,128)(2,1)}), bf16[4,528,256]{2,1,0:T(8,128)(2,1)S(1)}, u32[]{:S(2)}, u32[]{:S(2)}) async-start(bf16[4,528,256]{2,1,0:T(8,128)(2,1)} %get-tuple-element.11), calls=%async_computation | async-start | bytes 2162688 | tf_op jit(solution)/shard_map/all_to_all | solution.py:426
  7.6 31.0 %collective-permute-start = (bf16[528,256]{1,0:T(8,128)(2,1)}, bf16[528,256]{1,0:T(8,128)(2,1)S(1)}, u32[]{:S(2)}, u32[]{:S(2)}) collective-permute-start(bf16[528,256]{1,0:T(8,128)(2,1)} %get-tuple-element.13), channel_id=1, source_target_pairs={{0,1},{1,2},{2,3},{3,4},{4,5},{5,6},{6,7},{8,9},{9,10},{10,11},{11... | collective-permute-start | bytes 811016 | tf_op jit(solution)/shard_map/ppermute | solution.py:434
  11.7 26.8 %collective-permute-start.1 = (bf16[528,256]{1,0:T(8,128)(2,1)}, bf16[528,256]{1,0:T(8,128)(2,1)S(1)}, u32[]{:S(2)}, u32[]{:S(2)}) collective-permute-start(bf16[528,256]{1,0:T(8,128)(2,1)} %get-tuple-element.14), channel_id=1, source_target_pairs={{0,9},{1,10},{2,11},{3,12},{4,13},{5,14},{6,15},{8,1},{9,2},{10,3}... | collective-permute-start | bytes 811016 | tf_op jit(solution)/shard_map/ppermute | solution.py:434
  15.0 23.6 %collective-permute-start.2 = (bf16[528,256]{1,0:T(8,128)(2,1)}, bf16[528,256]{1,0:T(8,128)(2,1)S(1)}, u32[]{:S(2)}, u32[]{:S(2)}) collective-permute-start(bf16[528,256]{1,0:T(8,128)(2,1)} %get-tuple-element.15), channel_id=1, source_target_pairs={{0,17},{1,18},{2,19},{3,20},{4,21},{5,22},{6,23},{8,25},{9,26},{10... | collective-permute-start | bytes 811016 | tf_op jit(solution)/shard_map/ppermute | solution.py:434
  19.5 19.0 %copy-start = (s32[4]{0:T(128)S(1)}, s32[4]{0:T(128)}, u32[]{:S(2)}) copy-start(s32[4]{0:T(128)} %refs_0_.3) | copy-start | bytes 52
  19.5 19.0 %collective-permute-start.3 = (bf16[528,256]{1,0:T(8,128)(2,1)}, bf16[528,256]{1,0:T(8,128)(2,1)S(1)}, u32[]{:S(2)}, u32[]{:S(2)}) collective-permute-start(bf16[528,256]{1,0:T(8,128)(2,1)} %get-tuple-element.16), channel_id=1, source_target_pairs={{0,25},{1,26},{2,27},{3,28},{4,29},{5,30},{6,31},{8,17},{9,18},{10... | collective-permute-start | bytes 811016 | tf_op jit(solution)/shard_map/ppermute | solution.py:434
